TPU v7x, 32 devices: a whole 2x2x4 slice. The times are simulated.
32 devices in a mesh: grp: 2 (over y), freq: 4 (over z), tm: 2 (over x), pol: 2 (over core).
Axes of the slice: x: 2, y: 2, z: 4, core: 2. Of those that a mesh axis runs over, the one named last changes fastest.
Arguments:
- voltages: bfloat16 [2, 8, 1024, 4, 2, 256], P('pol', ('grp', 'freq'), 'tm'), parts along dimension 1, may hold values from -6 to 6
- feed_gains: float32 [8, 2, 4, 2, 256], P(('grp', 'freq'), 'pol'), parts along dimension 0, may hold values from -5 to 5
- owner_table: int32 [64], replicated, may hold values from 0 to 3, as said below
- keep_flags: int32 [1024], replicated, may hold values 0 or 1
Outputs:
- owned: bfloat16 [128, 64, 2048], P(('grp', 'tm', 'pol'), None, 'freq'), parts along dimension 0
There are 2 independent parts, one for each index of `grp`. A program takes and returns all parts, laid end to end along the dimension named above; an argument that names none is the same for every part. Nothing has to cross between parts.
Inputs may be any that keep to these rules, and one draw needn't show every extreme that they name: `owner_table`: each index of freq owns from 0 to 32 beam sets; one owns exactly 32.
All inputs are finite; a program needn't handle non-finite values.
Results may differ from a plain program's by a relative error of at most 0.0058.
Values may be sent and summed in bfloat16 or wider, within the bound.
A program may use at most 64 MiB of HBM per device.

v0:
```python
import functools

import jax
import jax.numpy as jnp
import ml_dtypes
import numpy as np
from jax import lax
from jax.experimental import pallas as pl
from jax.experimental.pallas import tpu as pltpu
from jax.sharding import PartitionSpec as P

NS = 256
CYL = 4
UPCH = 16
TAPS = 16
SET_BEAMS = 16
GROUP = 8
ROWS = GROUP * UPCH
WIDE = GROUP * UPCH * 2
BEAMS = CYL * NS


def window_taps():
    span = TAPS * UPCH
    steps = np.arange(span, dtype=np.float64)
    weights = np.sinc((steps - (span - 1) / 2.0) / UPCH) * np.sin(np.pi * (steps + 0.5) / span) ** 2
    weights = weights / np.sqrt(np.sum(weights * weights))
    return weights.reshape(TAPS, UPCH)


def filter_table():
    window = window_taps()
    span = GROUP + 16
    angle = 2.0 * np.pi * (np.arange(UPCH)[:, None] * np.arange(UPCH)[None, :] % UPCH) / UPCH
    cosine, sine = np.cos(angle), np.sin(angle)
    table = np.zeros((2, GROUP, UPCH, span, UPCH, 2))
    for frame in range(GROUP):
        for tap in range(TAPS):
            at = frame + 1 + tap
            table[0, frame, :, at, :, 0] = window[tap] * cosine
            table[0, frame, :, at, :, 1] = window[tap] * sine
            table[1, frame, :, at, :, 0] = -window[tap] * sine
            table[1, frame, :, at, :, 1] = window[tap] * cosine
    table = table.reshape(2 * ROWS, span * UPCH * 2).astype(np.float32)
    return table.astype(ml_dtypes.bfloat16)


def beam_matrix():
    rows = np.arange(NS)
    phase = rows[:, None] * rows[None, :] % NS
    angle = np.float32(2.0 * np.pi) * phase.astype(np.float32) / np.float32(NS)
    scale = np.float32(1.0 / np.sqrt(NS))
    cosine = np.cos(angle) * scale
    sine = np.sin(angle) * scale
    upper = np.concatenate([cosine, -sine], axis=1)
    lower = np.concatenate([sine, cosine], axis=1)
    return np.concatenate([upper, lower], axis=0).astype(ml_dtypes.bfloat16)


def kernel(
    n_freq, n_tm, groups, n_sets, x_ref, gain_ref, owner_ref, keep_ref, filt_ref, beam_ref, out_ref,
    xbuf, part, powers, arrived, place, outgoing,
    load_sem, halo_send, halo_recv, pol_send, pol_recv, set_send, set_recv, own_sem,
):
    freq = lax.axis_index("freq")
    tm = lax.axis_index("tm")
    pol = lax.axis_index("pol")
    half = groups // 2
    most = 2 * n_sets // n_freq
    columns = most * SET_BEAMS
    span = n_freq * columns

    loads = []
    for chunk in range(groups):
        load = pltpu.make_async_copy(x_ref.at[chunk], xbuf.at[chunk + 2], load_sem.at[chunk])
        load.start()
        loads.append(load)

    barrier = pltpu.get_barrier_semaphore()
    pl.semaphore_signal(barrier, inc=1, device_id={"pol": 1 - pol}, device_id_type=pl.DeviceIdType.MESH)
    for step in range(1, n_freq):
        pl.semaphore_signal(
            barrier, inc=1, device_id={"freq": lax.rem(freq + step, n_freq)}, device_id_type=pl.DeviceIdType.MESH
        )
    for step in range(1, n_tm):
        pl.semaphore_signal(
            barrier, inc=1, device_id={"tm": lax.rem(tm + step, n_tm)}, device_id_type=pl.DeviceIdType.MESH
        )
    pl.semaphore_wait(barrier, n_freq + n_tm - 1)

    def halo(chunk):
        return pltpu.make_async_remote_copy(
            src_ref=x_ref.at[groups - 2 + chunk],
            dst_ref=xbuf.at[chunk],
            send_sem=halo_send.at[chunk],
            recv_sem=halo_recv.at[chunk],
            device_id={"tm": lax.rem(tm + 1, n_tm)},
            device_id_type=pl.DeviceIdType.MESH,
        )

    @pl.when(tm < n_tm - 1)
    def _():
        halo(1).start()
        halo(0).start()

    @pl.when(tm == 0)
    def _():
        xbuf[0] = jnp.zeros(xbuf.shape[1:], xbuf.dtype)
        xbuf[1] = jnp.zeros(xbuf.shape[1:], xbuf.dtype)

    owner_row = owner_ref[...].astype(jnp.float32)
    s_row = lax.broadcasted_iota(jnp.int32, (n_sets, n_sets), 0)
    s_col = lax.broadcasted_iota(jnp.int32, (n_sets, n_sets), 1)
    spread = jnp.broadcast_to(owner_row, (n_sets, n_sets))
    owner_col = jnp.sum(jnp.where(s_row == s_col, spread, 0.0), axis=1, keepdims=True)
    same = jnp.logical_and(spread == owner_col, s_col < s_row)
    rank = jnp.sum(jnp.where(same, 1.0, 0.0), axis=1, keepdims=True)
    slot = (owner_col * most + rank).astype(jnp.int32)
    column = lax.broadcasted_iota(jnp.int32, (n_sets, span), 1)
    set_at = lax.broadcasted_iota(jnp.int32, (n_sets, span), 0)
    match = slot == column // SET_BEAMS
    beam_at = jnp.where(match, (set_at * SET_BEAMS + column % SET_BEAMS + 1).astype(jnp.float32), 0.0)
    beam_of = jnp.sum(beam_at, axis=0, keepdims=True).astype(jnp.int32) - 1
    keep = keep_ref[...].astype(jnp.float32)

    @pl.loop(0, BEAMS // 16)
    def _(step):
        first = pl.multiple_of(step * 16, 16)
        beam = lax.broadcasted_iota(jnp.int32, (16, span), 0) + first
        place[pl.ds(first, 16), :] = jnp.where(beam == beam_of, 1.0, 0.0).astype(jnp.bfloat16)

    def to_partner(g):
        return pltpu.make_async_remote_copy(
            src_ref=powers.at[g],
            dst_ref=arrived.at[g % half],
            send_sem=pol_send.at[g % half],
            recv_sem=pol_recv.at[g % half],
            device_id={"pol": 1 - pol},
            device_id_type=pl.DeviceIdType.MESH,
        )

    def to_owner(g, owner):
        rows = pl.ds(pl.multiple_of((g % half) * GROUP, GROUP), GROUP)
        return pltpu.make_async_remote_copy(
            src_ref=outgoing.at[g % half, owner],
            dst_ref=out_ref.at[rows, freq],
            send_sem=set_send.at[g % half, owner],
            recv_sem=set_recv.at[g % half, freq],
            device_id={"freq": owner},
            device_id_type=pl.DeviceIdType.MESH,
        )

    def from_source(slot_at, source):
        rows = pl.ds(slot_at * GROUP, GROUP)
        return pltpu.make_async_remote_copy(
            src_ref=outgoing.at[slot_at, source],
            dst_ref=out_ref.at[rows, source],
            send_sem=set_send.at[slot_at, source],
            recv_sem=set_recv.at[slot_at, source],
            device_id={"freq": source},
            device_id_type=pl.DeviceIdType.MESH,
        )

    def own_copy(g):
        rows = pl.ds(pl.multiple_of((g % half) * GROUP, GROUP), GROUP)
        return pltpu.make_async_copy(outgoing.at[g % half, freq], out_ref.at[rows, freq], own_sem.at[g % half])

    for load in loads:
        load.wait()

    @pl.loop(0, groups)
    def _(index):
        g = groups - 1 - index

        @pl.when(jnp.logical_and(g < 2, tm > 0))
        def _():
            halo(g).wait_recv()

        for y in range(CYL):
            total = jnp.dot(filt_ref[:, 0:WIDE], xbuf[g, y], preferred_element_type=jnp.float32)
            total += jnp.dot(filt_ref[:, WIDE : 2 * WIDE], xbuf[g + 1, y], preferred_element_type=jnp.float32)
            total += jnp.dot(filt_ref[:, 2 * WIDE : 3 * WIDE], xbuf[g + 2, y], preferred_element_type=jnp.float32)
            real, imag = total[:ROWS], total[ROWS:]
            gain_real = gain_ref[2 * y : 2 * y + 1, :]
            gain_imag = gain_ref[2 * y + 1 : 2 * y + 2, :]
            cal_real = (real * gain_real - imag * gain_imag).astype(jnp.bfloat16)
            cal_imag = (real * gain_imag + imag * gain_real).astype(jnp.bfloat16)
            calibrated = jnp.concatenate([cal_real, cal_imag], axis=1)
            part[y] = jnp.dot(calibrated, beam_ref[...], preferred_element_type=jnp.float32)

        @pl.loop(0, ROWS // 16)
        def _(step):
            rows = pl.ds(pl.multiple_of(step * 16, 16), 16)
            re = [part[y, rows, 0:NS] for y in range(CYL)]
            im = [part[y, rows, NS : 2 * NS] for y in range(CYL)]
            sum_re, sum_im = re[0] + re[2], im[0] + im[2]
            odd_re, odd_im = re[1] + re[3], im[1] + im[3]
            dif_re, dif_im = re[0] - re[2], im[0] - im[2]
            cross_re, cross_im = re[1] - re[3], im[1] - im[3]
            formed = (
                (sum_re + odd_re, sum_im + odd_im),
                (dif_re + cross_im, dif_im - cross_re),
                (sum_re - odd_re, sum_im - odd_im),
                (dif_re - cross_im, dif_im + cross_re),
            )
            for e, (f_re, f_im) in enumerate(formed):
                value = 0.25 * (f_re * f_re + f_im * f_im)
                powers[g, rows, e * NS : (e + 1) * NS] = value.astype(jnp.bfloat16)

        mine = g // half == pol

        @pl.when(jnp.logical_not(mine))
        def _():
            to_partner(g).start()

        @pl.when(mine)
        def _():
            to_partner(g).wait_recv()
            both = powers[g].astype(jnp.float32) + arrived[g % half].astype(jnp.float32)
            intensity = both.astype(jnp.bfloat16) * keep.astype(jnp.bfloat16)
            for owner in range(n_freq):
                block = jnp.dot(
                    intensity,
                    place[:, owner * columns : (owner + 1) * columns],
                    preferred_element_type=jnp.float32,
                )
                outgoing[g % half, owner] = block.astype(jnp.bfloat16).reshape(GROUP, UPCH, columns)
            for step in range(1, n_freq):
                to_owner(g, lax.rem(freq + step, n_freq)).start()
            own_copy(g).start()

    for slot_at in range(half):
        own_copy(slot_at).wait()
        to_partner(slot_at).wait_send()
        for step in range(1, n_freq):
            peer = lax.rem(freq + step, n_freq)
            from_source(slot_at, peer).wait_send()
            from_source(slot_at, peer).wait_recv()

    @pl.when(tm < n_tm - 1)
    def _():
        halo(0).wait_send()
        halo(1).wait_send()


def per_device(n_freq, n_tm, voltages, feed_gains, owner_table, keep_flags):
    samples = voltages.shape[2]
    groups = samples // (UPCH * GROUP)
    n_sets = owner_table.shape[0]
    columns = 2 * n_sets // n_freq * SET_BEAMS
    span = n_freq * columns
    half = groups // 2
    x = voltages.reshape(groups, GROUP * UPCH, CYL, 2, NS)
    x = x.transpose(0, 2, 1, 3, 4).reshape(groups, CYL, WIDE, NS)
    gains = feed_gains.reshape(CYL * 2, NS)
    vmem = pl.BlockSpec(memory_space=pltpu.VMEM)
    hbm = pl.BlockSpec(memory_space=pl.ANY)
    dma = pltpu.SemaphoreType.DMA
    out = pl.pallas_call(
        functools.partial(kernel, n_freq, n_tm, groups, n_sets),
        out_shape=jax.ShapeDtypeStruct((half * GROUP, n_freq, UPCH, columns), jnp.bfloat16),
        in_specs=[hbm, vmem, vmem, vmem, vmem, vmem],
        out_specs=hbm,
        scratch_shapes=[
            pltpu.VMEM((groups + 2, CYL, WIDE, NS), jnp.bfloat16),
            pltpu.VMEM((CYL, ROWS, 2 * NS), jnp.float32),
            pltpu.VMEM((groups, ROWS, BEAMS), jnp.bfloat16),
            pltpu.VMEM((half, ROWS, BEAMS), jnp.bfloat16),
            pltpu.VMEM((BEAMS, span), jnp.bfloat16),
            pltpu.VMEM((half, n_freq, GROUP, UPCH, columns), jnp.bfloat16),
            dma((groups,)),
            dma((2,)),
            dma((2,)),
            dma((half,)),
            dma((half,)),
            dma((half, n_freq)),
            dma((half, n_freq)),
            dma((half,)),
        ],
        compiler_params=pltpu.CompilerParams(
            collective_id=0, has_side_effects=True, vmem_limit_bytes=48 * 1024 * 1024
        ),
    )(
        x,
        gains,
        owner_table.reshape(1, n_sets),
        keep_flags.reshape(1, BEAMS),
        jnp.asarray(filter_table()),
        jnp.asarray(beam_matrix()),
    )
    return out.reshape(half * GROUP, n_freq * UPCH, columns)


def solution(mesh):
    return jax.shard_map(
        functools.partial(per_device, mesh.shape["freq"], mesh.shape["tm"]),
        mesh=mesh,
        in_specs=(
            P("pol", ("grp", "freq"), "tm", None, None, None),
            P(("grp", "freq"), "pol", None, None, None),
            P(),
            P(),
        ),
        out_specs=P(("grp", "tm", "pol"), None, "freq"),
        check_vma=False,
    )
```

profile of v0, /device:TPU:10, one launch (start us, length us, event | category | flops | bytes accessed | tf_op | source)
XLA Modules:
  0.0 45.9 jit_solution(13850189785979321030)
XLA Ops:
  0.0 4.9 %copy.9 = bf16[4,128,4,2,256]{4,3,1,2,0:T(2,128)(2,1)} copy(bf16[4,128,4,2,256]{4,3,2,1,0:T(2,128)(2,1)} %bitcast.11) | data formatting | bytes 4194304 | tf_op jit(solution)/shard_map/reshape | solution.py:253
  4.9 0.0 copy-start.4
  4.9 0.0 copy-start
  4.9 0.0 copy-start.1
  4.9 0.0 copy-start.2
  5.0 0.0 copy-start.3
  5.0 2.8 %reshape.19.x_ref = bf16[4,4,256,256]{3,2,1,0:T(8,128)(2,1)S(1)} reshape(bf16[4,4,128,2,256]{4,3,2,1,0:T(2,128)(2,1)} %bitcast.10) | data formatting | bytes 4194304 | tf_op jit(solution)/shard_map/reshape | solution.py:254
  7.8 0.0 copy-done.4
  7.8 0.0 copy-done
  7.8 0.0 copy-done.1
  7.8 0.0 copy-done.2
  7.9 0.0 copy-done.3
  7.9 37.1 %shard_map.64 = bf16[16,4,16,512]{3,2,1,0:T(8,128)(2,1)S(1)} custom-call(bf16[4,4,256,256]{3,2,1,0:T(8,128)(2,1)S(1)} %reshape.19.x_ref, f32[8,256]{1,0:T(8,128)S(1)} %reshape.20.gain_ref, s32[1,64]{1,0:T(1,128)S(1)} %bitcast.9, s32[1,1024]{1,0:T(1,128)S(1)} %bitcast.8, bf16[256,768]{1,0:T(8,128)(2,1)S(1)} %copy-done.1, bf16[512,512]{1,0:T(8,128)(2,1)S(1)} %copy-done), custom_call_target="tpu_custom_call" | custom-call | tf_op jit(solution)/shard_map/pallas_call | solution.py:259
  45.0 1.0 %copy.11 = bf16[16,64,512]{2,1,0:T(8,128)(2,1)} copy(bf16[16,64,512]{2,1,0:T(8,128)(2,1)S(1)} %bitcast.7) | data formatting | bytes 2097152
  (1 shorter events, 0.0 us)
Async XLA Ops:
  4.9 2.9 %copy-start.4 = (f32[1,1,4,2,256]{4,3,2,1,0:T(2,128)S(1)}, f32[1,1,4,2,256]{4,3,2,1,0:T(2,128)}, u32[]{:S(2)}) copy-start(f32[1,1,4,2,256]{4,3,2,1,0:T(2,128)} %param.7) | copy-start | bytes 24580
  4.9 2.9 %copy-start = (bf16[512,512]{1,0:T(8,128)(2,1)S(1)}, bf16[512,512]{1,0:T(8,128)(2,1)}, u32[]{:S(2)}) copy-start(bf16[512,512]{1,0:T(8,128)(2,1)} %constant.5.clone.beam_ref) | copy-start | bytes 1572868
  4.9 2.9 %copy-start.1 = (bf16[256,768]{1,0:T(8,128)(2,1)S(1)}, bf16[256,768]{1,0:T(8,128)(2,1)}, u32[]{:S(2)}) copy-start(bf16[256,768]{1,0:T(8,128)(2,1)} %constant.4.clone.filt_ref) | copy-start | bytes 1179652
  4.9 2.9 %copy-start.2 = (s32[1024]{0:T(1024)S(1)}, s32[1024]{0:T(1024)}, u32[]{:S(2)}) copy-start(s32[1024]{0:T(1024)} %param.9) | copy-start | bytes 12292
  5.0 2.9 %copy-start.3 = (s32[64]{0:T(128)S(1)}, s32[64]{0:T(128)}, u32[]{:S(2)}) copy-start(s32[64]{0:T(128)} %param.8) | copy-start | bytes 772
where the time goes:
time: 46.1 us; the launch traced here: 45.9 us
  Pallas kernels  37.1 us (80%)
  local copies, waits for them, and re-layouts  8.77 us (19%)
    pallas_call x1, Pallas kernels, per_device(): pl.pallas_call(functools.partial(kernel, n_freq, n_tm, groups, n_sets), o...  37.1 us
    reshape x1, local copies, waits for them, and re-layouts, per_device(): x = voltages.reshape(groups, GROUP * UPCH, CYL, 2, NS)  4.94 us
    reshape x1, local copies, waits for them, and re-layouts, per_device(): x = x.transpose(0, 2, 1, 3, 4).reshape(groups, CYL, WIDE, NS)  2.83 us
    unnamed x11, local copies, waits for them, and re-layouts  0.99 us

commit v1 on v0

--- a/solution.py
+++ b/solution.py
@@ -59,7 +59,7 @@
 
 def kernel(
     n_freq, n_tm, groups, n_sets, x_ref, gain_ref, owner_ref, keep_ref, filt_ref, beam_ref, out_ref,
-    xbuf, part, powers, arrived, place, outgoing,
+    raw, xbuf, part, powers, arrived, place, outgoing,
     load_sem, halo_send, halo_recv, pol_send, pol_recv, set_send, set_recv, own_sem,
 ):
     freq = lax.axis_index("freq")
@@ -72,7 +72,7 @@
 
     loads = []
     for chunk in range(groups):
-        load = pltpu.make_async_copy(x_ref.at[chunk], xbuf.at[chunk + 2], load_sem.at[chunk])
+        load = pltpu.make_async_copy(x_ref.at[chunk], raw.at[chunk + 2], load_sem.at[chunk])
         load.start()
         loads.append(load)
 
@@ -89,24 +89,32 @@
     pl.semaphore_wait(barrier, n_freq + n_tm - 1)
 
     def halo(chunk):
+        first = UPCH * (1 - chunk)
+        rows = pl.ds(first, ROWS - first)
         return pltpu.make_async_remote_copy(
-            src_ref=x_ref.at[groups - 2 + chunk],
-            dst_ref=xbuf.at[chunk],
+            src_ref=x_ref.at[groups - 2 + chunk, rows],
+            dst_ref=raw.at[chunk, rows],
             send_sem=halo_send.at[chunk],
             recv_sem=halo_recv.at[chunk],
             device_id={"tm": lax.rem(tm + 1, n_tm)},
             device_id_type=pl.DeviceIdType.MESH,
         )
 
+    def reorder(chunk):
+        for y in range(CYL):
+            xbuf[chunk, y] = raw[chunk, :, y].reshape(WIDE, NS)
+
     @pl.when(tm < n_tm - 1)
     def _():
         halo(1).start()
         halo(0).start()
 
+    raw[0, 0:UPCH] = jnp.zeros((UPCH, CYL, 2, NS), raw.dtype)
+
     @pl.when(tm == 0)
     def _():
-        xbuf[0] = jnp.zeros(xbuf.shape[1:], xbuf.dtype)
-        xbuf[1] = jnp.zeros(xbuf.shape[1:], xbuf.dtype)
+        raw[0, UPCH:] = jnp.zeros((ROWS - UPCH, CYL, 2, NS), raw.dtype)
+        raw[1] = jnp.zeros((ROWS, CYL, 2, NS), raw.dtype)
 
     owner_row = owner_ref[...].astype(jnp.float32)
     s_row = lax.broadcasted_iota(jnp.int32, (n_sets, n_sets), 0)
@@ -167,14 +175,22 @@
 
     for load in loads:
         load.wait()
+    reorder(groups)
+    reorder(groups + 1)
 
     @pl.loop(0, groups)
     def _(index):
         g = groups - 1 - index
 
-        @pl.when(jnp.logical_and(g < 2, tm > 0))
+        @pl.when(jnp.logical_and(g == 1, tm > 0))
         def _():
-            halo(g).wait_recv()
+            halo(1).wait_recv()
+
+        @pl.when(jnp.logical_and(g == 0, tm > 0))
+        def _():
+            halo(0).wait_recv()
+
+        reorder(g)
 
         for y in range(CYL):
             total = jnp.dot(filt_ref[:, 0:WIDE], xbuf[g, y], preferred_element_type=jnp.float32)
@@ -250,8 +266,7 @@
     columns = 2 * n_sets // n_freq * SET_BEAMS
     span = n_freq * columns
     half = groups // 2
-    x = voltages.reshape(groups, GROUP * UPCH, CYL, 2, NS)
-    x = x.transpose(0, 2, 1, 3, 4).reshape(groups, CYL, WIDE, NS)
+    x = voltages.reshape(groups, ROWS, CYL, 2, NS)
     gains = feed_gains.reshape(CYL * 2, NS)
     vmem = pl.BlockSpec(memory_space=pltpu.VMEM)
     hbm = pl.BlockSpec(memory_space=pl.ANY)
@@ -262,6 +277,7 @@
         in_specs=[hbm, vmem, vmem, vmem, vmem, vmem],
         out_specs=hbm,
         scratch_shapes=[
+            pltpu.VMEM((groups + 2, ROWS, CYL, 2, NS), jnp.bfloat16),
             pltpu.VMEM((groups + 2, CYL, WIDE, NS), jnp.bfloat16),
             pltpu.VMEM((CYL, ROWS, 2 * NS), jnp.float32),
             pltpu.VMEM((groups, ROWS, BEAMS), jnp.bfloat16),

time: 46.1 us -> 42.7 us (0.926)
  local copies, waits for them, and re-layouts: 8.77 us -> 6.65 us
  Pallas kernels: 37.1 us -> 35.7 us
    reshape x2 -> x0, local copies, waits for them, and re-layouts: 7.77 us -> none  [the longest x1 4.94 us: per_device(): x = voltages.reshape(groups, GROUP * UPCH, CYL, 2, NS)]
    unnamed x11, local copies, waits for them, and re-layouts: 0.99 us -> 5.94 us
    pallas_call x1, Pallas kernels: 37.1 us -> 35.7 us  [per_device(): pl.pallas_call(functools.partial(kernel, n_freq, n_tm, groups, n_sets), o...]
    reshape x1, local copies, waits for them, and re-layouts: 0.01 us -> 0.71 us  [per_device(): gains = feed_gains.reshape(CYL * 2, NS)]
where the time goes in v1:
time: 42.7 us; the launch traced here: 42.4 us
  Pallas kernels  35.7 us (84%)
  local copies, waits for them, and re-layouts  6.65 us (16%)
    pallas_call x1, Pallas kernels, per_device(): pl.pallas_call(functools.partial(kernel, n_freq, n_tm, groups, n_sets), o...  35.7 us
    unnamed x11, local copies, waits for them, and re-layouts  5.94 us

profile of v1, /device:TPU:10, one launch (start us, length us, event | category | flops | bytes accessed | tf_op | source)
XLA Modules:
  0.0 42.4 jit_solution(2446158617703879073)
XLA Ops:
  0.0 0.7 %reshape.16.gain_ref = f32[8,256]{1,0:T(8,128)S(1)} reshape(f32[1,1,4,2,256]{4,3,2,1,0:T(2,128)} %param.7) | data formatting | bytes 16384 | tf_op jit(solution)/shard_map/reshape | solution.py:270
  0.7 0.0 copy-start
  0.7 1.6 %copy-done = bf16[1,1,512,4,2,256]{5,4,3,2,1,0:T(2,128)(2,1)S(1)} copy-done((bf16[1,1,512,4,2,256]{5,4,3,2,1,0:T(2,128)(2,1)S(1)}, bf16[1,1,512,4,2,256]{5,4,3,2,1,0:T(2,128)(2,1)}, u32[]{:S(2)}) %copy-start) | copy-done | bytes 2097176
  2.3 0.0 copy-start.1
  2.3 1.0 %copy-done.1 = bf16[512,512]{1,0:T(8,128)(2,1)S(1)} copy-done((bf16[512,512]{1,0:T(8,128)(2,1)S(1)}, bf16[512,512]{1,0:T(8,128)(2,1)}, u32[]{:S(2)}) %copy-start.1) | copy-done | bytes 524312
  3.3 0.0 copy-start.2
  3.3 1.0 %copy-done.2 = bf16[256,768]{1,0:T(8,128)(2,1)S(1)} copy-done((bf16[256,768]{1,0:T(8,128)(2,1)S(1)}, bf16[256,768]{1,0:T(8,128)(2,1)}, u32[]{:S(2)}) %copy-start.2) | copy-done | bytes 393240
  4.3 0.0 copy-start.3
  4.3 0.7 %copy-done.3 = s32[1024]{0:T(1024)S(1)} copy-done((s32[1024]{0:T(1024)S(1)}, s32[1024]{0:T(1024)}, u32[]{:S(2)}) %copy-start.3) | copy-done | bytes 4120
  5.0 0.0 copy-start.4
  5.0 0.7 %copy-done.4 = s32[64]{0:T(128)S(1)} copy-done((s32[64]{0:T(128)S(1)}, s32[64]{0:T(128)}, u32[]{:S(2)}) %copy-start.4) | copy-done | bytes 280
  5.7 35.7 %shard_map.64 = bf16[16,4,16,512]{3,2,1,0:T(8,128)(2,1)S(1)} custom-call(bf16[4,128,4,2,256]{4,3,2,1,0:T(2,128)(2,1)S(1)} %bitcast.5, f32[8,256]{1,0:T(8,128)S(1)} %reshape.16.gain_ref, s32[1,64]{1,0:T(1,128)S(1)} %bitcast.7, s32[1,1024]{1,0:T(1,128)S(1)} %bitcast.6, bf16[256,768]{1,0:T(8,128)(2,1)S(1)} %copy-done.2, bf16[512,512]{1,0:T(8,128)(2,1)S(1)} %copy-done.1), custom_call_target="tpu_custom_call" | custom-call | tf_op jit(solution)/shard_map/pallas_call | solution.py:274
  41.4 1.0 %copy.8 = bf16[16,64,512]{2,1,0:T(8,128)(2,1)} copy(bf16[16,64,512]{2,1,0:T(8,128)(2,1)S(1)} %bitcast.4) | data formatting | bytes 2097152
Async XLA Ops:
  0.7 1.6 %copy-start = (bf16[1,1,512,4,2,256]{5,4,3,2,1,0:T(2,128)(2,1)S(1)}, bf16[1,1,512,4,2,256]{5,4,3,2,1,0:T(2,128)(2,1)}, u32[]{:S(2)}) copy-start(bf16[1,1,512,4,2,256]{5,4,3,2,1,0:T(2,128)(2,1)} %param.6) | copy-start | bytes 6291460
  2.3 1.0 %copy-start.1 = (bf16[512,512]{1,0:T(8,128)(2,1)S(1)}, bf16[512,512]{1,0:T(8,128)(2,1)}, u32[]{:S(2)}) copy-start(bf16[512,512]{1,0:T(8,128)(2,1)} %constant.5.clone.beam_ref) | copy-start | bytes 1572868
  3.3 1.0 %copy-start.2 = (bf16[256,768]{1,0:T(8,128)(2,1)S(1)}, bf16[256,768]{1,0:T(8,128)(2,1)}, u32[]{:S(2)}) copy-start(bf16[256,768]{1,0:T(8,128)(2,1)} %constant.4.clone.filt_ref) | copy-start | bytes 1179652
  4.3 0.7 %copy-start.3 = (s32[1024]{0:T(1024)S(1)}, s32[1024]{0:T(1024)}, u32[]{:S(2)}) copy-start(s32[1024]{0:T(1024)} %param.9) | copy-start | bytes 12292
  5.0 0.7 %copy-start.4 = (s32[64]{0:T(128)S(1)}, s32[64]{0:T(128)}, u32[]{:S(2)}) copy-start(s32[64]{0:T(128)} %param.8) | copy-start | bytes 772

commit v2 on v0

v2 whole, which is shorter than its diff:
```python
import functools

import jax
import jax.numpy as jnp
import ml_dtypes
import numpy as np
from jax import lax
from jax.experimental import pallas as pl
from jax.experimental.pallas import tpu as pltpu
from jax.sharding import PartitionSpec as P

NS = 256
CYL = 4
UPCH = 16
TAPS = 16
SET_BEAMS = 16
GROUP = 8
ROWS = GROUP * UPCH
WIDE = GROUP * UPCH * 2
BEAMS = CYL * NS


def window_taps():
    span = TAPS * UPCH
    steps = np.arange(span, dtype=np.float64)
    weights = np.sinc((steps - (span - 1) / 2.0) / UPCH) * np.sin(np.pi * (steps + 0.5) / span) ** 2
    weights = weights / np.sqrt(np.sum(weights * weights))
    return weights.reshape(TAPS, UPCH)


def filter_table():
    window = window_taps()
    span = GROUP + 16
    angle = 2.0 * np.pi * (np.arange(UPCH)[:, None] * np.arange(UPCH)[None, :] % UPCH) / UPCH
    cosine, sine = np.cos(angle), np.sin(angle)
    table = np.zeros((2, GROUP, UPCH, span, UPCH, 2))
    for frame in range(GROUP):
        for tap in range(TAPS):
            at = frame + 1 + tap
            table[0, frame, :, at, :, 0] = window[tap] * cosine
            table[0, frame, :, at, :, 1] = window[tap] * sine
            table[1, frame, :, at, :, 0] = -window[tap] * sine
            table[1, frame, :, at, :, 1] = window[tap] * cosine
    table = table.reshape(2 * ROWS, span * UPCH * 2).astype(np.float32)
    return table.astype(ml_dtypes.bfloat16)


def beam_matrix():
    rows = np.arange(NS)
    phase = rows[:, None] * rows[None, :] % NS
    angle = np.float32(2.0 * np.pi) * phase.astype(np.float32) / np.float32(NS)
    scale = np.float32(1.0 / np.sqrt(NS))
    cosine = np.cos(angle) * scale
    sine = np.sin(angle) * scale
    upper = np.concatenate([cosine, -sine], axis=1)
    lower = np.concatenate([sine, cosine], axis=1)
    return np.concatenate([upper, lower], axis=0).astype(ml_dtypes.bfloat16)


def kernel(
    n_freq, n_tm, groups, n_sets, x_ref, gain_hbm, owner_hbm, keep_hbm, filt_hbm, beam_hbm, out_ref,
    gain_ref, owner_ref, keep_ref, filt_ref, beam_ref,
    raw, xbuf, part, powers, arrived, place, outgoing, handed, given,
    load_sem, table_sem, halo_send, halo_recv, pol_send, pol_recv, hand_send, hand_recv, set_send, set_recv, own_sem,
):
    freq = lax.axis_index("freq")
    tm = lax.axis_index("tm")
    pol = lax.axis_index("pol")
    has_next = tm < n_tm - 1
    has_prev = tm > 0
    half = groups // 2
    most = 2 * n_sets // n_freq
    columns = most * SET_BEAMS
    span = n_freq * columns
    mesh_id = pl.DeviceIdType.MESH

    barrier = pltpu.get_barrier_semaphore()
    pl.semaphore_signal(barrier, inc=1, device_id={"pol": 1 - pol}, device_id_type=mesh_id)
    for step in range(1, n_freq):
        pl.semaphore_signal(barrier, inc=1, device_id={"freq": lax.rem(freq + step, n_freq)}, device_id_type=mesh_id)
    for step in range(1, n_tm):
        pl.semaphore_signal(barrier, inc=1, device_id={"tm": lax.rem(tm + step, n_tm)}, device_id_type=mesh_id)

    pairs = ((owner_hbm, owner_ref), (keep_hbm, keep_ref), (filt_hbm, filt_ref), (gain_hbm, gain_ref), (beam_hbm, beam_ref))
    tables = [pltpu.make_async_copy(src, dst, table_sem.at[i]) for i, (src, dst) in enumerate(pairs)]
    loads = [pltpu.make_async_copy(x_ref.at[i], raw.at[i + 2], load_sem.at[i]) for i in range(groups)]
    tables[0].start()
    tables[1].start()
    for load in loads[::-1]:
        load.start()
    for table in tables[2:]:
        table.start()

    pl.semaphore_wait(barrier, n_freq + n_tm - 1)

    def forward():
        rows = pl.ds(UPCH, ROWS - UPCH)
        return pltpu.make_async_remote_copy(
            src_ref=x_ref.at[groups - 1, rows],
            dst_ref=raw.at[1, rows],
            send_sem=halo_send.at[0],
            recv_sem=halo_recv.at[0],
            device_id={"tm": lax.rem(tm + 1, n_tm)},
            device_id_type=mesh_id,
        )

    def backward():
        return pltpu.make_async_remote_copy(
            src_ref=x_ref.at[0],
            dst_ref=raw.at[groups + 2],
            send_sem=halo_send.at[1],
            recv_sem=halo_recv.at[1],
            device_id={"tm": lax.rem(tm + n_tm - 1, n_tm)},
            device_id_type=mesh_id,
        )

    def hand_over():
        return pltpu.make_async_remote_copy(
            src_ref=handed,
            dst_ref=given,
            send_sem=hand_send,
            recv_sem=hand_recv,
            device_id={"tm": lax.rem(tm + 1, n_tm)},
            device_id_type=mesh_id,
        )

    def reorder(chunk):
        for y in range(CYL):
            xbuf[chunk, y] = raw[chunk, :, y].reshape(WIDE, NS)

    @pl.when(has_next)
    def _():
        forward().start()

    @pl.when(has_prev)
    def _():
        backward().start()

    raw[1, 0:UPCH] = jnp.zeros((UPCH, CYL, 2, NS), raw.dtype)

    @pl.when(tm == 0)
    def _():
        raw[0] = jnp.zeros((ROWS, CYL, 2, NS), raw.dtype)
        raw[1, UPCH:] = jnp.zeros((ROWS - UPCH, CYL, 2, NS), raw.dtype)

    tables[0].wait()
    tables[1].wait()
    owner_row = owner_ref[...].astype(jnp.float32)
    s_row = lax.broadcasted_iota(jnp.int32, (n_sets, n_sets), 0)
    s_col = lax.broadcasted_iota(jnp.int32, (n_sets, n_sets), 1)
    spread = jnp.broadcast_to(owner_row, (n_sets, n_sets))
    owner_col = jnp.sum(jnp.where(s_row == s_col, spread, 0.0), axis=1, keepdims=True)
    same = jnp.logical_and(spread == owner_col, s_col < s_row)
    rank = jnp.sum(jnp.where(same, 1.0, 0.0), axis=1, keepdims=True)
    slot = (owner_col * most + rank).astype(jnp.int32)
    column = lax.broadcasted_iota(jnp.int32, (n_sets, span), 1)
    set_at = lax.broadcasted_iota(jnp.int32, (n_sets, span), 0)
    match = slot == column // SET_BEAMS
    beam_at = jnp.where(match, (set_at * SET_BEAMS + column % SET_BEAMS + 1).astype(jnp.float32), 0.0)
    beam_of = jnp.sum(beam_at, axis=0, keepdims=True).astype(jnp.int32) - 1

    @pl.loop(0, BEAMS // 16)
    def _(step):
        first = pl.multiple_of(step * 16, 16)
        beam = lax.broadcasted_iota(jnp.int32, (16, span), 0) + first
        place[pl.ds(first, 16), :] = jnp.where(beam == beam_of, 1.0, 0.0).astype(jnp.bfloat16)

    def to_partner(g, at):
        return pltpu.make_async_remote_copy(
            src_ref=powers.at[g],
            dst_ref=arrived.at[at],
            send_sem=pol_send.at[at],
            recv_sem=pol_recv.at[at],
            device_id={"pol": 1 - pol},
            device_id_type=mesh_id,
        )

    def to_owner(at, owner):
        rows = pl.ds(at * GROUP, GROUP)
        return pltpu.make_async_remote_copy(
            src_ref=outgoing.at[at, owner],
            dst_ref=out_ref.at[rows, freq],
            send_sem=set_send.at[at, owner],
            recv_sem=set_recv.at[at, freq],
            device_id={"freq": owner},
            device_id_type=mesh_id,
        )

    def from_source(at, source):
        rows = pl.ds(at * GROUP, GROUP)
        return pltpu.make_async_remote_copy(
            src_ref=outgoing.at[at, source],
            dst_ref=out_ref.at[rows, source],
            send_sem=set_send.at[at, source],
            recv_sem=set_recv.at[at, source],
            device_id={"freq": source},
            device_id_type=mesh_id,
        )

    def own_copy(at):
        rows = pl.ds(at * GROUP, GROUP)
        return pltpu.make_async_copy(outgoing.at[at, freq], out_ref.at[rows, freq], own_sem.at[at])

    def form_powers(g):
        for y in range(CYL):
            total = jnp.dot(filt_ref[:, 0:WIDE], xbuf[g, y], preferred_element_type=jnp.float32)
            total += jnp.dot(filt_ref[:, WIDE : 2 * WIDE], xbuf[g + 1, y], preferred_element_type=jnp.float32)
            total += jnp.dot(filt_ref[:, 2 * WIDE : 3 * WIDE], xbuf[g + 2, y], preferred_element_type=jnp.float32)
            real, imag = total[:ROWS], total[ROWS:]
            gain_real = gain_ref[y, 0:1, :]
            gain_imag = gain_ref[y, 1:2, :]
            cal_real = (real * gain_real - imag * gain_imag).astype(jnp.bfloat16)
            cal_imag = (real * gain_imag + imag * gain_real).astype(jnp.bfloat16)
            calibrated = jnp.concatenate([cal_real, cal_imag], axis=1)
            part[y] = jnp.dot(calibrated, beam_ref[...], preferred_element_type=jnp.float32)

        @pl.loop(0, ROWS // 16)
        def _(step):
            rows = pl.ds(pl.multiple_of(step * 16, 16), 16)
            re = [part[y, rows, 0:NS] for y in range(CYL)]
            im = [part[y, rows, NS : 2 * NS] for y in range(CYL)]
            sum_re, sum_im = re[0] + re[2], im[0] + im[2]
            odd_re, odd_im = re[1] + re[3], im[1] + im[3]
            dif_re, dif_im = re[0] - re[2], im[0] - im[2]
            cross_re, cross_im = re[1] - re[3], im[1] - im[3]
            formed = (
                (sum_re + odd_re, sum_im + odd_im),
                (dif_re + cross_im, dif_im - cross_re),
                (sum_re - odd_re, sum_im - odd_im),
                (dif_re - cross_im, dif_im + cross_re),
            )
            for e, (f_re, f_im) in enumerate(formed):
                value = 0.25 * (f_re * f_re + f_im * f_im)
                powers[g, rows, e * NS : (e + 1) * NS] = value.astype(jnp.bfloat16)

    def both_pols(g, at):
        to_partner(g, at).wait_recv()
        both = powers[g].astype(jnp.float32) + arrived[at].astype(jnp.float32)
        return both.astype(jnp.bfloat16) * keep_ref[...].astype(jnp.bfloat16)

    def regroup(intensity, at):
        for step in range(n_freq):
            owner = lax.rem(freq + step, n_freq) if step else freq
            first = pl.multiple_of(owner * columns, columns)
            block = jnp.dot(intensity, place[:, pl.ds(first, columns)], preferred_element_type=jnp.float32)
            outgoing[at, owner] = block.astype(jnp.bfloat16).reshape(GROUP, UPCH, columns)
            if step:
                to_owner(at, owner).start()
            else:
                own_copy(at).start()

    for load in loads:
        load.wait()
    for table in tables[2:]:
        table.wait()
    reorder(groups)
    reorder(groups + 1)

    @pl.loop(0, groups - 1)
    def _(index):
        g = groups - 1 - index

        @pl.when(jnp.logical_and(g == 1, has_prev))
        def _():
            forward().wait_recv()

        reorder(g)
        form_powers(g)
        mine = g // half == pol

        @pl.when(jnp.logical_not(mine))
        def _():
            to_partner(g, g % half).start()

        @pl.when(mine)
        def _():
            regroup(both_pols(g, g % half), g % half)

    @pl.loop(0, 2)
    def _(index):
        g = groups * (1 - index)
        at = half * (1 - index)

        @pl.when(jnp.logical_or(jnp.logical_and(index == 0, has_next), jnp.logical_and(index == 1, tm == 0)))
        def _():
            @pl.when(index == 0)
            def _():
                backward().wait_recv()
                reorder(groups + 2)

            @pl.when(index == 1)
            def _():
                reorder(0)
                reorder(1)

            form_powers(g)

            @pl.when(pol == 1)
            def _():
                to_partner(g, at).start()

            @pl.when(pol == 0)
            def _():
                @pl.when(index == 0)
                def _():
                    handed[...] = both_pols(g, at)
                    hand_over().start()

                @pl.when(index == 1)
                def _():
                    given[...] = both_pols(g, at)

        @pl.when(jnp.logical_and(index == 1, pol == 0))
        def _():
            @pl.when(has_prev)
            def _():
                hand_over().wait_recv()

            regroup(given[...], 0)

    for at in range(half):
        own_copy(at).wait()
        for step in range(1, n_freq):
            peer = lax.rem(freq + step, n_freq)
            from_source(at, peer).wait_send()
            from_source(at, peer).wait_recv()
        if at:
            to_partner(at, at).wait_send()

    @pl.when(jnp.logical_or(pol == 0, tm == 0))
    def _():
        to_partner(0, 0).wait_send()

    @pl.when(has_next)
    def _():
        forward().wait_send()

        @pl.when(pol == 1)
        def _():
            to_partner(groups, half).wait_send()

        @pl.when(pol == 0)
        def _():
            hand_over().wait_send()

    @pl.when(has_prev)
    def _():
        backward().wait_send()


def per_device(n_freq, n_tm, voltages, feed_gains, owner_table, keep_flags):
    samples = voltages.shape[2]
    groups = samples // (UPCH * GROUP)
    n_sets = owner_table.shape[0]
    columns = 2 * n_sets // n_freq * SET_BEAMS
    span = n_freq * columns
    half = groups // 2
    x = voltages.reshape(groups, ROWS, CYL, 2, NS)
    gains = feed_gains.reshape(CYL, 2, NS)
    hbm = pl.BlockSpec(memory_space=pl.ANY)
    dma = pltpu.SemaphoreType.DMA
    out = pl.pallas_call(
        functools.partial(kernel, n_freq, n_tm, groups, n_sets),
        out_shape=jax.ShapeDtypeStruct((half * GROUP, n_freq, UPCH, columns), jnp.bfloat16),
        in_specs=[hbm] * 6,
        out_specs=hbm,
        scratch_shapes=[
            pltpu.VMEM((CYL, 2, NS), jnp.float32),
            pltpu.VMEM((1, n_sets), jnp.int32),
            pltpu.VMEM((1, BEAMS), jnp.int32),
            pltpu.VMEM((2 * ROWS, 3 * WIDE), jnp.bfloat16),
            pltpu.VMEM((2 * NS, 2 * NS), jnp.bfloat16),
            pltpu.VMEM((groups + 3, ROWS, CYL, 2, NS), jnp.bfloat16),
            pltpu.VMEM((groups + 3, CYL, WIDE, NS), jnp.bfloat16),
            pltpu.VMEM((CYL, ROWS, 2 * NS), jnp.float32),
            pltpu.VMEM((groups + 1, ROWS, BEAMS), jnp.bfloat16),
            pltpu.VMEM((half + 1, ROWS, BEAMS), jnp.bfloat16),
            pltpu.VMEM((BEAMS, span), jnp.bfloat16),
            pltpu.VMEM((half, n_freq, GROUP, UPCH, columns), jnp.bfloat16),
            pltpu.VMEM((ROWS, BEAMS), jnp.bfloat16),
            pltpu.VMEM((ROWS, BEAMS), jnp.bfloat16),
            dma((groups,)),
            dma((5,)),
            dma((2,)),
            dma((2,)),
            dma((half + 1,)),
            dma((half + 1,)),
            dma(()),
            dma(()),
            dma((half, n_freq)),
            dma((half, n_freq)),
            dma((half,)),
        ],
        compiler_params=pltpu.CompilerParams(
            collective_id=0, has_side_effects=True, vmem_limit_bytes=58 * 1024 * 1024
        ),
    )(
        x,
        gains,
        owner_table.reshape(1, n_sets),
        keep_flags.reshape(1, BEAMS),
        jnp.asarray(filter_table()),
        jnp.asarray(beam_matrix()),
    )
    return out.reshape(half * GROUP, n_freq * UPCH, columns)


def solution(mesh):
    return jax.shard_map(
        functools.partial(per_device, mesh.shape["freq"], mesh.shape["tm"]),
        mesh=mesh,
        in_specs=(
            P("pol", ("grp", "freq"), "tm", None, None, None),
            P(("grp", "freq"), "pol", None, None, None),
            P(),
            P(),
        ),
        out_specs=P(("grp", "tm", "pol"), None, "freq"),
        check_vma=False,
    )
```

time: 46.1 us -> 36.7 us (0.80)
  the two profiles are of different devices: /device:TPU:10 before, /device:TPU:0 now
where the time goes in v2:
time: 36.7 us; the launch traced here: 36.5 us
  Pallas kernels  34.2 us (93%)
  local copies, waits for them, and re-layouts  2.29 us (6%)
    pallas_call x1, Pallas kernels, per_device(): pl.pallas_call(functools.partial(kernel, n_freq, n_tm, groups, n_sets), o...  34.2 us
    unnamed x1, local copies, waits for them, and re-layouts  2.29 us

profile of v2, /device:TPU:0, one launch (start us, length us, event | category | flops | bytes accessed | tf_op | source)
XLA Modules:
  0.0 36.5 jit_solution(1659721933726634248)
XLA Ops:
  0.0 34.2 %shard_map.64 = bf16[16,4,16,512]{3,2,1,0:T(8,128)(2,1)} custom-call(bf16[4,128,4,2,256]{4,3,2,1,0:T(2,128)(2,1)} %bitcast.6, f32[4,2,256]{2,1,0:T(2,128)} %bitcast.7, s32[1,64]{1,0:T(1,128)} %bitcast.9, s32[1,1024]{1,0:T(1,128)} %bitcast.8, bf16[256,768]{1,0:T(8,128)(2,1)} %constant.4.clone.filt_hbm, bf16[512,512]{1,0:T(8,128)(2,1)} %constant.5.clone.beam_hbm), custom_call_target="tpu_custom_call" | custom-call | tf_op jit(solution)/shard_map/pallas_call | solution.py:362
  34.2 2.3 %copy.8 = bf16[16,64,512]{2,1,0:T(8,128)(2,1)} copy(bf16[16,64,512]{2,1,0:T(8,128)(2,1)} %bitcast.5) | data formatting | bytes 2097152
